TPU v7x, 1024 devices: a whole 4x8x16 slice. The times are simulated.
1024 devices in a mesh: group: 32 (over z, core), bal: 32 (over x, y).
Axes of the slice: x: 4, y: 8, z: 16, core: 2. Of those that a mesh axis runs over, the one named last changes fastest.
Arguments:
- query_rows: bfloat16 [2048, 128, 512], P(('group', 'bal')), may hold values from -6 to 6
- key_rows: bfloat16 [2048, 128, 512], P(('group', 'bal')), may hold values from -6 to 6
- value_rows: bfloat16 [2048, 128, 512], P(('group', 'bal')), may hold values from -6 to 6
- gate_rows: bfloat16 [2048, 128, 512], P(('group', 'bal')), may hold values from -6 to 6
- upstream: bfloat16 [2048, 128, 1024], P(('group', 'bal')), may hold values from -6 to 6
- lengths: int32 [2048], P('group'), may hold values from 0 to 128
- route_plan: int32 [1024], P('group'), may hold values from 0 to 31
- out_weight: bfloat16 [512, 1024], replicated, may hold values from -0.25 to 0.25
- prune_scores: float32 [512, 1024], P('bal', 'group'), may hold values from -6 to 6
Outputs:
- grad_query: bfloat16 [2048, 128, 512], P(('group', 'bal'))
- grad_key: bfloat16 [2048, 128, 512], P(('group', 'bal'))
- grad_value: bfloat16 [2048, 128, 512], P(('group', 'bal'))
- grad_gate: bfloat16 [2048, 128, 512], P(('group', 'bal'))
- weight_grad: float32 [512, 1024], P('bal', 'group')
- new_scores: float32 [512, 1024], P('bal', 'group')
All inputs are finite; a program needn't handle non-finite values.
Results may differ from a plain program's by a relative error of at most 0.0059.
Values may be sent and summed in bfloat16 or wider, within the bound.
No kernel may reach another device: no remote copies, remote signals or barrier semaphores. Data moves between devices by JAX's collectives and lax.ppermute only.
A program may use at most 32 MiB of HBM per device.

v0:
```python
import math

import jax
import jax.numpy as jnp
import numpy as np
from jax import lax
from jax.sharding import PartitionSpec as P

HEAD = 128


def shortened(shard):

    def short(part):
        return part.astype(jnp.bfloat16) if part.dtype == jnp.float32 else part

    return jax.tree.map(short, shard)


def from_partner(block, axis, bit):
    count = lax.axis_size(axis)
    route = []
    for low in range(count):
        high = low | 1 << bit
        if high != low and high < count:
            route += [(low, high), (high, low)]
    return lax.ppermute(block, axis, route)


def routing_slot_table(
    split_portions, device_route_table, slot_total_count, segment_count, transfer_buffer
):
    slot_ids = jnp.arange(slot_total_count, dtype=jnp.int32)
    for exchange_bit_position in range(segment_count):
        choose = device_route_table // slot_total_count**exchange_bit_position % slot_total_count
        departing_tiles = tuple(
            (lax.dynamic_index_in_dim(piece, choose, 0, keepdims=False) for piece in split_portions)
        )
        received_tiles = transfer_buffer(departing_tiles, exchange_bit_position)
        chosen = (slot_ids == choose)[:, None, None]
        split_portions = tuple(
            (
                jnp.where(chosen, arrived[None], piece)
                for arrived, piece in zip(received_tiles, split_portions)
            )
        )
    return split_portions


def route_lengths(length_table, plan_row, slot_total_count, segment_count):
    bal_count = length_table.shape[0]
    slot_ids = jnp.arange(slot_total_count, dtype=jnp.int32)
    for exchange_bit_position in range(segment_count):
        partners = np.arange(bal_count) ^ 1 << exchange_bit_position
        choose = plan_row // slot_total_count**exchange_bit_position % slot_total_count
        departing_tiles = jnp.take_along_axis(length_table, choose[:, None], axis=1)[:, 0]
        length_table = jnp.where(
            slot_ids[None, :] == choose[:, None], departing_tiles[partners][:, None], length_table
        )
    return length_table


def tile_backward(query_rows, key_rows, value_rows, gate_rows, upstream, lengths, out_weight):
    slot_total_count, tile_len, feat_width = query_rows.shape
    head_count = feat_width // HEAD
    head_shape = (slot_total_count, tile_len, head_count, HEAD)
    score_scale = 1.0 / math.sqrt(HEAD)
    positions = jnp.arange(tile_len, dtype=jnp.int32)
    live_rows = positions[None, :] < lengths[:, None]
    causal = positions[:, None] >= positions[None, :]
    pair_mask = (causal[None] & live_rows[:, None, :] & live_rows[:, :, None]).astype(jnp.float32)[
        :, None
    ]
    query_heads = query_rows.reshape(head_shape)
    key_heads = key_rows.reshape(head_shape)
    value_heads = value_rows.reshape(head_shape)
    logits = (
        jnp.einsum("sihd,sjhd->shij", query_heads, key_heads, preferred_element_type=jnp.float32)
        * score_scale
    )
    logit_sig = jax.nn.sigmoid(logits)
    attention = (logits * logit_sig / tile_len * pair_mask).astype(jnp.bfloat16)
    mixed_rows = jnp.einsum(
        "shij,sjhd->sihd", attention, value_heads, preferred_element_type=jnp.float32
    )
    mixed_rows = mixed_rows.reshape(slot_total_count, tile_len, feat_width)
    row_mean = jnp.mean(mixed_rows, axis=-1, keepdims=True)
    centred = mixed_rows - row_mean
    variance = jnp.mean(centred * centred, axis=-1, keepdims=True)
    inv_std = lax.rsqrt(variance + 1e-05)
    normed = centred * inv_std
    gate_f = gate_rows.astype(jnp.float32)
    gated_rows = (normed * gate_f).astype(jnp.bfloat16)
    grad_gated = jnp.einsum("sie,we->siw", upstream, out_weight, preferred_element_type=jnp.float32)
    grad_gated = grad_gated * live_rows[:, :, None].astype(jnp.float32)
    grad_gate = (grad_gated * normed).astype(jnp.bfloat16)
    grad_normed = grad_gated * gate_f
    grad_mixed = inv_std * (
        grad_normed
        - jnp.mean(grad_normed, axis=-1, keepdims=True)
        - normed * jnp.mean(grad_normed * normed, axis=-1, keepdims=True)
    )
    grad_mixed = grad_mixed.astype(jnp.bfloat16).reshape(head_shape)
    grad_attention = jnp.einsum(
        "sihd,sjhd->shij", grad_mixed, value_heads, preferred_element_type=jnp.float32
    )
    grad_logits = (
        grad_attention * logit_sig * (1.0 + logits * (1.0 - logit_sig)) / tile_len * pair_mask
    ).astype(jnp.bfloat16)
    grad_value = jnp.einsum(
        "shij,sihd->sjhd", attention, grad_mixed, preferred_element_type=jnp.float32
    )
    grad_query = (
        jnp.einsum("shij,sjhd->sihd", grad_logits, key_heads, preferred_element_type=jnp.float32)
        * score_scale
    )
    grad_key = (
        jnp.einsum("shij,sihd->sjhd", grad_logits, query_heads, preferred_element_type=jnp.float32)
        * score_scale
    )
    flat_shape = (slot_total_count, tile_len, feat_width)
    partial_value = jnp.einsum(
        "siw,sie->we", gated_rows, upstream, preferred_element_type=jnp.float32
    )
    return (
        (
            grad_query.reshape(flat_shape).astype(jnp.bfloat16),
            grad_key.reshape(flat_shape).astype(jnp.bfloat16),
            grad_value.reshape(flat_shape).astype(jnp.bfloat16),
            grad_gate,
        ),
        partial_value,
    )


def per_device(
    query_rows,
    key_rows,
    value_rows,
    gate_rows,
    upstream,
    lengths,
    route_plan,
    out_weight,
    prune_scores,
):
    bal_count = lax.axis_size("bal")
    group_count = lax.axis_size("group")
    bal_pos = lax.axis_index("bal")
    group_pos = lax.axis_index("group")
    segment_count = bal_count.bit_length() - 1
    slot_total_count = query_rows.shape[0]
    tile_len = query_rows.shape[1]
    length_table = lengths.reshape(bal_count, slot_total_count)
    device_route_table = lax.dynamic_index_in_dim(route_plan, bal_pos, 0, keepdims=False)
    routed_table = route_lengths(length_table, route_plan, slot_total_count, segment_count)
    own_lengths = lax.dynamic_index_in_dim(routed_table, bal_pos, 0, keepdims=False)
    routed = routing_slot_table(
        (query_rows, key_rows, value_rows, gate_rows, upstream),
        device_route_table,
        slot_total_count,
        segment_count,
        lambda departing_tiles, exchange_bit_position: jax.tree.map(
            lambda part, own: part.astype(own.dtype),
            from_partner(shortened(departing_tiles), "bal", exchange_bit_position),
            departing_tiles,
        ),
    )
    grads, partial_value = tile_backward(
        routed[0], routed[1], routed[2], routed[3], routed[4], own_lengths, out_weight
    )
    row_block = lax.psum_scatter(partial_value, "bal", scatter_dimension=0, tiled=True)
    summed = lax.psum_scatter(row_block, "group", scatter_dimension=1, tiled=True)
    tokens_all = group_count * bal_count * slot_total_count * tile_len
    weight_grad = summed * (1.0 / math.sqrt(tokens_all))
    row_count = summed.shape[0]
    col_count = summed.shape[1]
    weight_block = lax.dynamic_slice(
        out_weight, (bal_pos * row_count, group_pos * col_count), (row_count, col_count)
    )
    new_scores = prune_scores - weight_block.astype(jnp.float32) * weight_grad
    return (grads[0], grads[1], grads[2], grads[3], weight_grad, new_scores)


def solution(mesh):
    placed = (
        P(("group", "bal"), None, None),
        P(("group", "bal"), None, None),
        P(("group", "bal"), None, None),
        P(("group", "bal"), None, None),
        P(("group", "bal"), None, None),
        P("group"),
        P("group"),
        P(),
        P("bal", "group"),
    )
    return jax.shard_map(
        per_device,
        mesh=mesh,
        in_specs=placed,
        out_specs=(
            P(("group", "bal"), None, None),
            P(("group", "bal"), None, None),
            P(("group", "bal"), None, None),
            P(("group", "bal"), None, None),
            P("bal", "group"),
            P("bal", "group"),
        ),
        check_vma=False,
    )
```

profile of v0, /device:TPU:6, one launch (start us, length us, event | category | flops | bytes accessed | tf_op | source)
XLA Modules:
  0.0 533.5 jit_solution(758845817801637402)
XLA Ops:
  11.3 3.5 collective-permute-start.20
  15.8 2.4 collective-permute-start.5
  19.0 3.5 collective-permute-start
  23.5 2.4 collective-permute-start.10
  26.8 3.5 collective-permute-start.15
  47.6 4.5 collective-permute-start.1
  54.4 4.5 collective-permute-start.6
  61.2 5.4 %collective-permute-done.1 = bf16[128,512]{1,0:T(8,128)(2,1)S(1)} collective-permute-done((bf16[128,512]{1,0:T(8,128)(2,1)S(1)}, bf16[128,512]{1,0:T(8,128)(2,1)S(1)}, u32[]{:S(2)}, u32[]{:S(2)}) %collective-permute-start.1) | collective-permute-done | bytes 131104 | tf_op jit(solution)/shard_map/ppermute | solution.py:27
  66.7 2.8 collective-permute-done.11
  69.5 2.8 collective-permute-done.6
  74.1 7.1 %collective-permute-start.2 = (bf16[128,512]{1,0:T(8,128)(2,1)S(1)}, bf16[128,512]{1,0:T(8,128)(2,1)S(1)}, u32[]{:S(2)}, u32[]{:S(2)}) collective-permute-start(bf16[128,512]{1,0:T(8,128)(2,1)S(1)} %dynamic-slice_bitcast_fusion.22), channel_id=1, source_target_pairs={{0,4},{4,0},{1,5},{5,1},{2,6},{6,2},{3,7},{7,3},{8,12},{12,8},{9,1... | collective-permute-start | bytes 393224 | tf_op jit(solution)/shard_map/ppermute | solution.py:27
  81.2 2.8 collective-permute-start.12
  84.0 6.9 %collective-permute-start.7 = (bf16[128,512]{1,0:T(8,128)(2,1)S(1)}, bf16[128,512]{1,0:T(8,128)(2,1)S(1)}, u32[]{:S(2)}, u32[]{:S(2)}) collective-permute-start(bf16[128,512]{1,0:T(8,128)(2,1)S(1)} %dynamic-slice_bitcast_fusion.17), channel_id=1, source_target_pairs={{0,4},{4,0},{1,5},{5,1},{2,6},{6,2},{3,7},{7,3},{8,12},{12,8},{9,1... | collective-permute-start | bytes 393224 | tf_op jit(solution)/shard_map/ppermute | solution.py:27
  90.9 2.8 collective-permute-start.22
  93.8 3.4 collective-permute-done.12
  97.2 5.3 %collective-permute-done.7 = bf16[128,512]{1,0:T(8,128)(2,1)S(1)} collective-permute-done((bf16[128,512]{1,0:T(8,128)(2,1)S(1)}, bf16[128,512]{1,0:T(8,128)(2,1)S(1)}, u32[]{:S(2)}, u32[]{:S(2)}) %collective-permute-start.7) | collective-permute-done | bytes 131104 | tf_op jit(solution)/shard_map/ppermute | solution.py:27
  102.6 2.8 collective-permute-done.22
  105.6 2.7 collective-permute-start.3
  108.4 3.1 collective-permute-start.13
  111.5 2.7 collective-permute-start.8
  114.3 3.1 collective-permute-start.23
  121.4 3.5 collective-permute-start.4
  124.9 3.8 collective-permute-start.14
  128.8 3.5 collective-permute-start.9
  132.5 5.6 %collective-permute-start.17 = (bf16[128,1024]{1,0:T(8,128)(2,1)S(1)}, bf16[128,1024]{1,0:T(8,128)(2,1)S(1)}, u32[]{:S(2)}, u32[]{:S(2)}) collective-permute-start(bf16[128,1024]{1,0:T(8,128)(2,1)S(1)} %dynamic-slice_bitcast_fusion.2), channel_id=1, source_target_pairs={{0,4},{4,0},{1,5},{5,1},{2,6},{6,2},{3,7},{7,3},{8,12},{12,8},{9,1... | collective-permute-start | bytes 786440 | tf_op jit(solution)/shard_map/ppermute | solution.py:27
  138.8 2.3 collective-permute-start.24
  141.9 8.1 %collective-permute-done.17 = bf16[128,1024]{1,0:T(8,128)(2,1)S(1)} collective-permute-done((bf16[128,1024]{1,0:T(8,128)(2,1)S(1)}, bf16[128,1024]{1,0:T(8,128)(2,1)S(1)}, u32[]{:S(2)}, u32[]{:S(2)}) %collective-permute-start.17) | collective-permute-done | bytes 262176 | tf_op jit(solution)/shard_map/ppermute | solution.py:27
  150.3 2.8 collective-permute-start.18
  154.4 5.6 %collective-permute-done.18 = bf16[128,1024]{1,0:T(8,128)(2,1)S(1)} collective-permute-done((bf16[128,1024]{1,0:T(8,128)(2,1)S(1)}, bf16[128,1024]{1,0:T(8,128)(2,1)S(1)}, u32[]{:S(2)}, u32[]{:S(2)}) %collective-permute-start.18) | collective-permute-done | bytes 262176 | tf_op jit(solution)/shard_map/ppermute | solution.py:27
  162.8 7.8 %collective-permute-done.19 = bf16[128,1024]{1,0:T(8,128)(2,1)S(1)} collective-permute-done((bf16[128,1024]{1,0:T(8,128)(2,1)S(1)}, bf16[128,1024]{1,0:T(8,128)(2,1)S(1)}, u32[]{:S(2)}, u32[]{:S(2)}) %collective-permute-start.19) | collective-permute-done | bytes 262176 | tf_op jit(solution)/shard_map/ppermute | solution.py:27
  178.4 231.2 %reduce-scatter.5.cloned.1.call-done = f32[16,1024]{1,0:T(8,128)} async-done(((f32[512,1024]{1,0:T(8,128)}), f32[16,1024]{1,0:T(8,128)}) %reduce-scatter.5.cloned.1.call-update) | async-done | bytes 65552 | tf_op jit(solution)/shard_map/reduce_scatter | solution.py:172
  412.6 111.9 %reduce-scatter.7.cloned.1.call-done = f32[32,16]{1,0:T(8,128)} async-done(((f32[1024,16]{1,0:T(8,128)}), f32[32,16]{1,0:T(8,128)}) %reduce-scatter.7.cloned.1.call-update) | async-done | bytes 2064
  (154 shorter events, 51.4 us)
Async XLA Ops:
  7.2 402.5 %reduce-scatter.5.cloned.1.call-start = ((), (), s32[]{:S(2)}) async-start(), calls=%async_computation.2 | async-start | bytes 2162688 | tf_op jit(solution)/shard_map/reduce_scatter | solution.py:172
  11.3 35.9 %collective-permute-start.20 = (bf16[128,512]{1,0:T(8,128)(2,1)S(1)}, bf16[128,512]{1,0:T(8,128)(2,1)S(1)}, u32[]{:S(2)}, u32[]{:S(2)}) collective-permute-start(bf16[128,512]{1,0:T(8,128)(2,1)S(1)} %dynamic-slice_bitcast_fusion.9), channel_id=1, source_target_pairs={{0,1},{1,0},{2,3},{3,2},{4,5},{5,4},{6,7},{7,6},{8,9},{9,8},{10,11... | collective-permute-start | bytes 393224 | tf_op jit(solution)/shard_map/ppermute | solution.py:27
  15.8 31.5 %collective-permute-start.5 = (bf16[128,512]{1,0:T(8,128)(2,1)S(1)}, bf16[128,512]{1,0:T(8,128)(2,1)S(1)}, u32[]{:S(2)}, u32[]{:S(2)}) collective-permute-start(bf16[128,512]{1,0:T(8,128)(2,1)S(1)} %dynamic-slice_bitcast_fusion.19), channel_id=1, source_target_pairs={{0,1},{1,0},{2,3},{3,2},{4,5},{5,4},{6,7},{7,6},{8,9},{9,8},{10,11... | collective-permute-start | bytes 393224 | tf_op jit(solution)/shard_map/ppermute | solution.py:27
  19.0 28.2 %collective-permute-start = (bf16[128,512]{1,0:T(8,128)(2,1)S(1)}, bf16[128,512]{1,0:T(8,128)(2,1)S(1)}, u32[]{:S(2)}, u32[]{:S(2)}) collective-permute-start(bf16[128,512]{1,0:T(8,128)(2,1)S(1)} %dynamic-slice_bitcast_fusion.24), channel_id=1, source_target_pairs={{0,1},{1,0},{2,3},{3,2},{4,5},{5,4},{6,7},{7,6},{8,9},{9,8},{10,11... | collective-permute-start | bytes 393224 | tf_op jit(solution)/shard_map/ppermute | solution.py:27
  23.5 23.8 %collective-permute-start.10 = (bf16[128,512]{1,0:T(8,128)(2,1)S(1)}, bf16[128,512]{1,0:T(8,128)(2,1)S(1)}, u32[]{:S(2)}, u32[]{:S(2)}) collective-permute-start(bf16[128,512]{1,0:T(8,128)(2,1)S(1)} %dynamic-slice_bitcast_fusion.14), channel_id=1, source_target_pairs={{0,1},{1,0},{2,3},{3,2},{4,5},{5,4},{6,7},{7,6},{8,9},{9,8},{10,11... | collective-permute-start | bytes 393224 | tf_op jit(solution)/shard_map/ppermute | solution.py:27
  26.8 90.6 %collective-permute-start.15 = (bf16[128,1024]{1,0:T(8,128)(2,1)S(1)}, bf16[128,1024]{1,0:T(8,128)(2,1)S(1)}, u32[]{:S(2)}, u32[]{:S(2)}) collective-permute-start(bf16[128,1024]{1,0:T(8,128)(2,1)S(1)} %dynamic-slice_bitcast_fusion.4), channel_id=1, source_target_pairs={{0,1},{1,0},{2,3},{3,2},{4,5},{5,4},{6,7},{7,6},{8,9},{9,8},{10,11... | collective-permute-start | bytes 786440 | tf_op jit(solution)/shard_map/ppermute | solution.py:27
  47.6 19.0 %collective-permute-start.1 = (bf16[128,512]{1,0:T(8,128)(2,1)S(1)}, bf16[128,512]{1,0:T(8,128)(2,1)S(1)}, u32[]{:S(2)}, u32[]{:S(2)}) collective-permute-start(bf16[128,512]{1,0:T(8,128)(2,1)S(1)} %dynamic-slice_bitcast_fusion.23), channel_id=1, source_target_pairs={{0,2},{2,0},{1,3},{3,1},{4,6},{6,4},{5,7},{7,5},{8,10},{10,8},{9,1... | collective-permute-start | bytes 393224 | tf_op jit(solution)/shard_map/ppermute | solution.py:27
  52.1 17.3 %collective-permute-start.11 = (bf16[128,512]{1,0:T(8,128)(2,1)S(1)}, bf16[128,512]{1,0:T(8,128)(2,1)S(1)}, u32[]{:S(2)}, u32[]{:S(2)}) collective-permute-start(bf16[128,512]{1,0:T(8,128)(2,1)S(1)} %dynamic-slice_bitcast_fusion.13), channel_id=1, source_target_pairs={{0,2},{2,0},{1,3},{3,1},{4,6},{6,4},{5,7},{7,5},{8,10},{10,8},{9,1... | collective-permute-start | bytes 393224 | tf_op jit(solution)/shard_map/ppermute | solution.py:27
  54.4 17.9 %collective-permute-start.6 = (bf16[128,512]{1,0:T(8,128)(2,1)S(1)}, bf16[128,512]{1,0:T(8,128)(2,1)S(1)}, u32[]{:S(2)}, u32[]{:S(2)}) collective-permute-start(bf16[128,512]{1,0:T(8,128)(2,1)S(1)} %dynamic-slice_bitcast_fusion.18), channel_id=1, source_target_pairs={{0,2},{2,0},{1,3},{3,1},{4,6},{6,4},{5,7},{7,5},{8,10},{10,8},{9,1... | collective-permute-start | bytes 393224 | tf_op jit(solution)/shard_map/ppermute | solution.py:27
  58.9 14.9 %collective-permute-start.21 = (bf16[128,512]{1,0:T(8,128)(2,1)S(1)}, bf16[128,512]{1,0:T(8,128)(2,1)S(1)}, u32[]{:S(2)}, u32[]{:S(2)}) collective-permute-start(bf16[128,512]{1,0:T(8,128)(2,1)S(1)} %dynamic-slice_bitcast_fusion.8), channel_id=1, source_target_pairs={{0,2},{2,0},{1,3},{3,1},{4,6},{6,4},{5,7},{7,5},{8,10},{10,8},{9,1... | collective-permute-start | bytes 393224 | tf_op jit(solution)/shard_map/ppermute | solution.py:27
  61.2 88.9 %copy-start.9 = (pred[2]{0:T(512)(128)(4,1)}, pred[2]{0:T(512)(128)(4,1)S(1)}, u32[]{:S(2)}) copy-start(pred[2]{0:T(512)(128)(4,1)S(1)} %iota_compare_fusion.8) | copy-start | bytes 10
  74.0 43.4 %copy-start = (bf16[2,128,1024]{2,1,0:T(8,128)(2,1)S(1)}, bf16[2,128,1024]{2,1,0:T(8,128)(2,1)}, u32[]{:S(2)}) copy-start(bf16[2,128,1024]{2,1,0:T(8,128)(2,1)} %param.25) | copy-start | bytes 1572868
  74.1 19.8 %collective-permute-start.2 = (bf16[128,512]{1,0:T(8,128)(2,1)S(1)}, bf16[128,512]{1,0:T(8,128)(2,1)S(1)}, u32[]{:S(2)}, u32[]{:S(2)}) collective-permute-start(bf16[128,512]{1,0:T(8,128)(2,1)S(1)} %dynamic-slice_bitcast_fusion.22), channel_id=1, source_target_pairs={{0,4},{4,0},{1,5},{5,1},{2,6},{6,2},{3,7},{7,3},{8,12},{12,8},{9,1... | collective-permute-start | bytes 393224 | tf_op jit(solution)/shard_map/ppermute | solution.py:27
  81.2 16.1 %collective-permute-start.12 = (bf16[128,512]{1,0:T(8,128)(2,1)S(1)}, bf16[128,512]{1,0:T(8,128)(2,1)S(1)}, u32[]{:S(2)}, u32[]{:S(2)}) collective-permute-start(bf16[128,512]{1,0:T(8,128)(2,1)S(1)} %dynamic-slice_bitcast_fusion.12), channel_id=1, source_target_pairs={{0,4},{4,0},{1,5},{5,1},{2,6},{6,2},{3,7},{7,3},{8,12},{12,8},{9,1... | collective-permute-start | bytes 393224 | tf_op jit(solution)/shard_map/ppermute | solution.py:27
  84.0 18.6 %collective-permute-start.7 = (bf16[128,512]{1,0:T(8,128)(2,1)S(1)}, bf16[128,512]{1,0:T(8,128)(2,1)S(1)}, u32[]{:S(2)}, u32[]{:S(2)}) collective-permute-start(bf16[128,512]{1,0:T(8,128)(2,1)S(1)} %dynamic-slice_bitcast_fusion.17), channel_id=1, source_target_pairs={{0,4},{4,0},{1,5},{5,1},{2,6},{6,2},{3,7},{7,3},{8,12},{12,8},{9,1... | collective-permute-start | bytes 393224 | tf_op jit(solution)/shard_map/ppermute | solution.py:27
  90.9 14.5 %collective-permute-start.22 = (bf16[128,512]{1,0:T(8,128)(2,1)S(1)}, bf16[128,512]{1,0:T(8,128)(2,1)S(1)}, u32[]{:S(2)}, u32[]{:S(2)}) collective-permute-start(bf16[128,512]{1,0:T(8,128)(2,1)S(1)} %dynamic-slice_bitcast_fusion.7), channel_id=1, source_target_pairs={{0,4},{4,0},{1,5},{5,1},{2,6},{6,2},{3,7},{7,3},{8,12},{12,8},{9,1... | collective-permute-start | bytes 393224 | tf_op jit(solution)/shard_map/ppermute | solution.py:27
  93.8 27.3 %copy-start.11 = (pred[2]{0:T(512)(128)(4,1)}, pred[2]{0:T(512)(128)(4,1)S(1)}, u32[]{:S(2)}) copy-start(pred[2]{0:T(512)(128)(4,1)S(1)} %iota_compare_fusion.9) | copy-start | bytes 10
  105.6 13.9 %collective-permute-start.3 = (bf16[128,512]{1,0:T(8,128)(2,1)S(1)}, bf16[128,512]{1,0:T(8,128)(2,1)S(1)}, u32[]{:S(2)}, u32[]{:S(2)}) collective-permute-start(bf16[128,512]{1,0:T(8,128)(2,1)S(1)} %dynamic-slice_bitcast_fusion.21), channel_id=1, source_target_pairs={{0,8},{8,0},{1,9},{9,1},{2,10},{10,2},{3,11},{11,3},{4,12},{12,4},... | collective-permute-start | bytes 393224 | tf_op jit(solution)/shard_map/ppermute | solution.py:27
  108.4 11.1 %collective-permute-start.13 = (bf16[128,512]{1,0:T(8,128)(2,1)S(1)}, bf16[128,512]{1,0:T(8,128)(2,1)S(1)}, u32[]{:S(2)}, u32[]{:S(2)}) collective-permute-start(bf16[128,512]{1,0:T(8,128)(2,1)S(1)} %dynamic-slice_bitcast_fusion.11), channel_id=1, source_target_pairs={{0,8},{8,0},{1,9},{9,1},{2,10},{10,2},{3,11},{11,3},{4,12},{12,4},... | collective-permute-start | bytes 393224 | tf_op jit(solution)/shard_map/ppermute | solution.py:27
  111.5 8.0 %collective-permute-start.8 = (bf16[128,512]{1,0:T(8,128)(2,1)S(1)}, bf16[128,512]{1,0:T(8,128)(2,1)S(1)}, u32[]{:S(2)}, u32[]{:S(2)}) collective-permute-start(bf16[128,512]{1,0:T(8,128)(2,1)S(1)} %dynamic-slice_bitcast_fusion.16), channel_id=1, source_target_pairs={{0,8},{8,0},{1,9},{9,1},{2,10},{10,2},{3,11},{11,3},{4,12},{12,4},... | collective-permute-start | bytes 393224 | tf_op jit(solution)/shard_map/ppermute | solution.py:27
  114.3 6.9 %collective-permute-start.23 = (bf16[128,512]{1,0:T(8,128)(2,1)S(1)}, bf16[128,512]{1,0:T(8,128)(2,1)S(1)}, u32[]{:S(2)}, u32[]{:S(2)}) collective-permute-start(bf16[128,512]{1,0:T(8,128)(2,1)S(1)} %dynamic-slice_bitcast_fusion.6), channel_id=1, source_target_pairs={{0,8},{8,0},{1,9},{9,1},{2,10},{10,2},{3,11},{11,3},{4,12},{12,4},... | collective-permute-start | bytes 393224 | tf_op jit(solution)/shard_map/ppermute | solution.py:27
  117.6 14.8 %collective-permute-start.16 = (bf16[128,1024]{1,0:T(8,128)(2,1)S(1)}, bf16[128,1024]{1,0:T(8,128)(2,1)S(1)}, u32[]{:S(2)}, u32[]{:S(2)}) collective-permute-start(bf16[128,1024]{1,0:T(8,128)(2,1)S(1)} %dynamic-slice_bitcast_fusion.3), channel_id=1, source_target_pairs={{0,2},{2,0},{1,3},{3,1},{4,6},{6,4},{5,7},{7,5},{8,10},{10,8},{9,1... | collective-permute-start | bytes 786440 | tf_op jit(solution)/shard_map/ppermute | solution.py:27
  121.4 19.7 %collective-permute-start.4 = (bf16[128,512]{1,0:T(8,128)(2,1)S(1)}, bf16[128,512]{1,0:T(8,128)(2,1)S(1)}, u32[]{:S(2)}, u32[]{:S(2)}) collective-permute-start(bf16[128,512]{1,0:T(8,128)(2,1)S(1)} %dynamic-slice_bitcast_fusion.20), channel_id=1, source_target_pairs={{0,16},{16,0},{1,17},{17,1},{2,18},{18,2},{3,19},{19,3},{4,20},{20... | collective-permute-start | bytes 393224 | tf_op jit(solution)/shard_map/ppermute | solution.py:27
  124.9 16.2 %collective-permute-start.14 = (bf16[128,512]{1,0:T(8,128)(2,1)S(1)}, bf16[128,512]{1,0:T(8,128)(2,1)S(1)}, u32[]{:S(2)}, u32[]{:S(2)}) collective-permute-start(bf16[128,512]{1,0:T(8,128)(2,1)S(1)} %dynamic-slice_bitcast_fusion.10), channel_id=1, source_target_pairs={{0,16},{16,0},{1,17},{17,1},{2,18},{18,2},{3,19},{19,3},{4,20},{20... | collective-permute-start | bytes 393224 | tf_op jit(solution)/shard_map/ppermute | solution.py:27
  128.8 12.3 %collective-permute-start.9 = (bf16[128,512]{1,0:T(8,128)(2,1)S(1)}, bf16[128,512]{1,0:T(8,128)(2,1)S(1)}, u32[]{:S(2)}, u32[]{:S(2)}) collective-permute-start(bf16[128,512]{1,0:T(8,128)(2,1)S(1)} %dynamic-slice_bitcast_fusion.15), channel_id=1, source_target_pairs={{0,16},{16,0},{1,17},{17,1},{2,18},{18,2},{3,19},{19,3},{4,20},{20... | collective-permute-start | bytes 393224 | tf_op jit(solution)/shard_map/ppermute | solution.py:27
  132.5 17.6 %collective-permute-start.17 = (bf16[128,1024]{1,0:T(8,128)(2,1)S(1)}, bf16[128,1024]{1,0:T(8,128)(2,1)S(1)}, u32[]{:S(2)}, u32[]{:S(2)}) collective-permute-start(bf16[128,1024]{1,0:T(8,128)(2,1)S(1)} %dynamic-slice_bitcast_fusion.2), channel_id=1, source_target_pairs={{0,4},{4,0},{1,5},{5,1},{2,6},{6,2},{3,7},{7,3},{8,12},{12,8},{9,1... | collective-permute-start | bytes 786440 | tf_op jit(solution)/shard_map/ppermute | solution.py:27
  138.8 23.9 %collective-permute-start.24 = (bf16[128,512]{1,0:T(8,128)(2,1)}, bf16[128,512]{1,0:T(8,128)(2,1)S(1)}, u32[]{:S(2)}, u32[]{:S(2)}) collective-permute-start(bf16[128,512]{1,0:T(8,128)(2,1)} %dynamic-slice_bitcast_fusion.5), channel_id=1, source_target_pairs={{0,16},{16,0},{1,17},{17,1},{2,18},{18,2},{3,19},{19,3},{4,20},{20... | collective-permute-start | bytes 393224 | tf_op jit(solution)/shard_map/ppermute | solution.py:27
  141.9 12.4 %copy-start.5 = (f32[2,4,128,128]{3,2,1,0:T(8,128)}, f32[2,4,128,128]{3,2,1,0:T(8,128)S(1)}, u32[]{:S(2)}) copy-start(f32[2,4,128,128]{3,2,1,0:T(8,128)S(1)} %convolution_multiply_fusion.4) | copy-start | bytes 1572868
  150.3 9.7 %collective-permute-start.18 = (bf16[128,1024]{1,0:T(8,128)(2,1)S(1)}, bf16[128,1024]{1,0:T(8,128)(2,1)S(1)}, u32[]{:S(2)}, u32[]{:S(2)}) collective-permute-start(bf16[128,1024]{1,0:T(8,128)(2,1)S(1)} %dynamic-slice_bitcast_fusion.1), channel_id=1, source_target_pairs={{0,8},{8,0},{1,9},{9,1},{2,10},{10,2},{3,11},{11,3},{4,12},{12,4},... | collective-permute-start | bytes 786440 | tf_op jit(solution)/shard_map/ppermute | solution.py:27
  160.3 10.3 %collective-permute-start.19 = (bf16[128,1024]{1,0:T(8,128)(2,1)S(1)}, bf16[128,1024]{1,0:T(8,128)(2,1)S(1)}, u32[]{:S(2)}, u32[]{:S(2)}) collective-permute-start(bf16[128,1024]{1,0:T(8,128)(2,1)S(1)} %dynamic-slice_bitcast_fusion), channel_id=1, source_target_pairs={{0,16},{16,0},{1,17},{17,1},{2,18},{18,2},{3,19},{19,3},{4,20},{20... | collective-permute-start | bytes 786440 | tf_op jit(solution)/shard_map/ppermute | solution.py:27
  172.6 352.0 %reduce-scatter.7.cloned.1.call-start = ((), (), s32[]{:S(2)}) async-start(), calls=%async_computation.3 | async-start | bytes 540672
  177.3 348.1 %copy-start.8 = (f32[16,32]{1,0:T(8,128)S(1)}, f32[16,32]{1,0:T(8,128)}, u32[]{:S(2)}) copy-start(f32[16,32]{1,0:T(8,128)} %param.29) | copy-start | bytes 6148
  (9 other events, 69.3 us)
Sparse Core Ops, SparseCore 0:
  172.7 236.9 reduce-scatter.4
  413.4 111.0 reduce-scatter.6
where the time goes:
time: 535 us; the launch traced here: 534 us
  waiting for transfers between devices  391 us (73%)
  starting transfers between devices  85.7 us (16%)
  local copies, waits for them, and re-layouts  21.9 us (4%)
  between operations  17.7 us (3%)
  other arithmetic  11.1 us (2%)
  matrix products  6.61 us (1%)
    reduce_scatter x1, waiting for transfers between devices, per_device(): lax.psum_scatter(partial_value, 'bal', scatter_dimension=0, tiled=True)  231 us
    unnamed x3, waiting for transfers between devices  112 us
    ppermute x25, starting transfers between devices, from_partner(): return lax.ppermute(block, axis, route)  85.6 us
    ppermute x25, waiting for transfers between devices, from_partner(): return lax.ppermute(block, axis, route)  47.3 us
  transfers between devices with their start and end apart: 27, of which 13 were waited for; matrix products, arithmetic and copies ran while one was open for 6% of the time, Pallas kernels for 0%

commit v1 on v0

v1 whole, which is shorter than its diff:
```python
import math

import jax
import jax.numpy as jnp
from jax import lax
from jax.experimental import pallas as pl
from jax.experimental.pallas import tpu as pltpu
from jax.sharding import PartitionSpec as P

HEAD = 128
STRIP = 16
SMALL = 16 * 2**20
BIG = 60 * 2**20


def dot(a, b, ca, cb):
    return lax.dot_general(a, b, (((ca,), (cb,)), ((), ())), preferred_element_type=jnp.float32)


def heads_of(width):
    return [slice(h * HEAD, (h + 1) * HEAD) for h in range(width // HEAD)]


def grad_kernel(len_ref, plan_ref, *refs):
    far, (pieces, keep_ref, send_ref, from_ref, block_ref), near = refs[:6], refs[6:11], refs[11:17]
    z_ref, sum_ref, sems = refs[17:]
    copies = [pltpu.make_async_copy(a, b, sems.at[i]) for i, (a, b) in enumerate(zip(far, near))]
    for copy in copies:
        copy.start()
    q, k, v, u, g, w = near
    count, slots = plan_ref.shape[0], q.shape[0]
    for i in range(count * slots):
        from_ref[i] = i
    for t in range(count.bit_length() - 1):
        for low in range(count):
            high = low | 1 << t
            if high != low:
                a = low * slots + ((plan_ref[low] >> t) & 1)
                b = high * slots + ((plan_ref[high] >> t) & 1)
                held, other = from_ref[a], from_ref[b]
                from_ref[a] = other
                from_ref[b] = held
    for copy in copies:
        copy.wait()
    pos, group = lax.axis_index("bal"), lax.axis_index("group")
    rows, width = q.shape[1:]
    strips, share = rows // STRIP, width // HEAD * STRIP
    scale = 1.0 / math.sqrt(HEAD)

    def put(which, tile, h, value):
        at = slice(tile * share + h * STRIP, tile * share + (h + 1) * STRIP)
        value = value.astype(jnp.bfloat16).reshape(strips, STRIP, HEAD)
        pieces[which * strips : (which + 1) * strips, at, :] = value

    row_ids = lax.broadcasted_iota(jnp.int32, (rows, rows), 0)
    col_ids = lax.broadcasted_iota(jnp.int32, (rows, rows), 1)
    for tile in range(slots):
        live = len_ref[pos * slots + tile]
        allowed = (col_ids <= row_ids) & (row_ids < live)
        logits, sigs, atts, mixed = [], [], [], []
        for at in heads_of(width):
            s = dot(q[tile, :, at], k[tile, :, at], 1, 1) * scale
            sig = jax.nn.sigmoid(s)
            a = jnp.where(allowed, s * sig * (1.0 / rows), 0.0).astype(jnp.bfloat16)
            logits.append(s)
            sigs.append(sig)
            atts.append(a)
            mixed.append(dot(a, v[tile, :, at], 1, 0))
        o = jnp.concatenate(mixed, axis=1)
        centred = o - jnp.mean(o, axis=-1, keepdims=True)
        inv_std = lax.rsqrt(jnp.mean(centred * centred, axis=-1, keepdims=True) + 1e-05)
        normed = centred * inv_std
        gate = u[tile].astype(jnp.float32)
        z_ref[tile] = (normed * gate).astype(jnp.bfloat16)
        row_live = lax.broadcasted_iota(jnp.int32, (rows, 1), 0) < live
        dz = jnp.where(row_live, dot(g[tile], w[...], 1, 1), 0.0)
        grad_gate = dz * normed
        dn = dz * gate
        do = inv_std * (
            dn
            - jnp.mean(dn, axis=-1, keepdims=True)
            - normed * jnp.mean(dn * normed, axis=-1, keepdims=True)
        )
        do = do.astype(jnp.bfloat16)
        for h, at in enumerate(heads_of(width)):
            put(0, tile, h, grad_gate[:, at])
            doh = do[:, at]
            put(1, tile, h, dot(atts[h], doh, 0, 0))
            da = dot(doh, v[tile, :, at], 1, 1)
            s, sig = logits[h], sigs[h]
            ds = jnp.where(allowed, da * sig * (1.0 + s * (1.0 - sig)) * (1.0 / rows), 0.0)
            ds = ds.astype(jnp.bfloat16)
            put(2, tile, h, dot(ds, k[tile, :, at], 1, 0) * scale)
            put(3, tile, h, dot(ds, q[tile, :, at], 0, 0) * scale)
    total = sum(dot(g[tile], z_ref[tile], 0, 0) for tile in range(slots))
    sum_ref[...] = total.reshape(sum_ref.shape)
    core = group & 1
    own, block = block_ref.shape
    for out, which in ((keep_ref, core), (send_ref, 1 - core)):
        half = sum_ref[:, which].reshape(width, width).T
        for c, at in enumerate(heads_of(width)):
            out[:, c * own : (c + 1) * own, :] = half[:, at].reshape(count, own, HEAD)
    wide = w.shape[1]
    pick = lax.broadcasted_iota(jnp.int32, (wide, block), 0) == (
        lax.broadcasted_iota(jnp.int32, (wide, block), 1) + group * block
    )
    lines = w[pl.ds(pl.multiple_of(pos * own, own), own), :]
    block_ref[...] = dot(lines, pick.astype(jnp.float32).astype(jnp.bfloat16), 1, 0)


def order_kernel(from_ref, strips_ref, out_ref, sum_ref):
    count, lines = out_ref.shape[:2]
    share = lines // 2
    for at in range(count):
        for slot in range(2):
            source = from_ref[at * 2 + slot]
            row = pl.multiple_of((source & 1) * share, share)
            out_ref[at, slot * share : (slot + 1) * share, :] = strips_ref[source >> 1, pl.ds(row, share), :]
    sum_ref[...] = jnp.sum(strips_ref[:, lines:, :].astype(jnp.float32), axis=0)


def place_kernel(factor, strips_ref, sums_ref, block_ref, prune_ref, *outs):
    slots, rows, width = outs[0].shape
    strips, share = rows // STRIP, width // HEAD * STRIP
    for which in range(4):
        for slot in range(slots):
            for h, at in enumerate(heads_of(width)):
                lines = slice(slot * share + h * STRIP, slot * share + (h + 1) * STRIP)
                got = strips_ref[which * strips : (which + 1) * strips, lines, :]
                outs[which][slot, :, at] = got.reshape(rows, HEAD)
    own, block = outs[4].shape
    first = (lax.axis_index("group") >> 1) * block
    lines = pl.ds(pl.multiple_of(first // HEAD * own, own), own)
    total = jnp.sum(sums_ref[:, lines, :], axis=0)
    total = pltpu.roll(total, (HEAD - first % HEAD) % HEAD, 1)
    weight_grad = total[:, :block] * factor
    outs[4][...] = weight_grad
    outs[5][...] = prune_ref[...] - block_ref[...] * weight_grad


def per_device(query, key, value, gate, upstream, lengths, plan, out_weight, prune_scores):
    bal_count, group_count = lax.axis_size("bal"), lax.axis_size("group")
    slots, rows, width = query.shape
    out_width = upstream.shape[2]
    strips, heads = rows // STRIP, width // HEAD
    chips, block = group_count // 2, out_width // group_count
    own, lines = width // bal_count, slots * heads * STRIP
    smem = pl.BlockSpec(memory_space=pltpu.SMEM)
    vmem = pl.BlockSpec(memory_space=pltpu.VMEM)
    hbm = pl.BlockSpec(memory_space=pltpu.HBM)
    far = (query, key, value, gate, upstream, out_weight)

    def shape(*dims, kind=jnp.float32):
        return jax.ShapeDtypeStruct(dims, kind)

    half = shape(bal_count, heads * own, HEAD)
    pieces, keep, send, sources, weight_block = pl.pallas_call(
        grad_kernel,
        out_shape=[
            shape(bal_count, lines + heads * own, HEAD, kind=jnp.bfloat16),
            half,
            half,
            shape(bal_count * slots, kind=jnp.int32),
            shape(own, block),
        ],
        in_specs=[smem] * 2 + [hbm] * 6,
        out_specs=[vmem] * 3 + [smem, vmem],
        scratch_shapes=[pltpu.VMEM(a.shape, a.dtype) for a in far]
        + [
            pltpu.VMEM((slots, rows, width), jnp.bfloat16),
            pltpu.VMEM((chips, 2, block, width), jnp.float32),
            pltpu.SemaphoreType.DMA((6,)),
        ],
        compiler_params=pltpu.CompilerParams(vmem_limit_bytes=BIG),
        cost_estimate=pl.CostEstimate(flops=800_000_000, bytes_accessed=8_000_000, transcendentals=131072),
        name="tile_grads",
    )(lengths, plan, *far)

    cores = [(i, i ^ 1) for i in range(group_count)]
    total = keep + lax.ppermute(send, "group", cores)
    pieces = lax.dynamic_update_slice(pieces, total.astype(pieces.dtype), (0, lines, 0))
    spread = lax.all_to_all(pieces, "bal", 0, 0, tiled=True)
    routed, part = pl.pallas_call(
        order_kernel,
        out_shape=[shape(bal_count, lines, HEAD, kind=jnp.bfloat16), shape(heads * own, HEAD)],
        in_specs=[smem, vmem],
        out_specs=[vmem, vmem],
        compiler_params=pltpu.CompilerParams(vmem_limit_bytes=SMALL),
        cost_estimate=pl.CostEstimate(flops=0, bytes_accessed=2_000_000, transcendentals=0),
        name="routed_order",
    )(sources, spread)

    home = lax.all_to_all(routed, "bal", 0, 0, tiled=True)
    along = [[2 * z + core for z in range(chips)] for core in range(2)]
    parts = lax.all_gather(part, "group", axis_index_groups=along)
    tokens_all = group_count * bal_count * slots * rows
    outs = pl.pallas_call(
        lambda *refs: place_kernel(1.0 / math.sqrt(tokens_all), *refs),
        out_shape=[shape(slots, rows, width, kind=jnp.bfloat16)] * 4 + [shape(own, block)] * 2,
        in_specs=[vmem] * 4,
        out_specs=[vmem] * 6,
        compiler_params=pltpu.CompilerParams(vmem_limit_bytes=SMALL),
        name="place_grads",
    )(home, parts, weight_block, prune_scores)
    return (outs[2], outs[3], outs[1], outs[0], outs[4], outs[5])


def solution(mesh):
    tiles = P(("group", "bal"), None, None)
    return jax.shard_map(
        per_device,
        mesh=mesh,
        in_specs=(tiles,) * 5 + (P("group"), P("group"), P(), P("bal", "group")),
        out_specs=(tiles,) * 4 + (P("bal", "group"),) * 2,
        check_vma=False,
    )
```

time: 535 us -> 121 us (0.23)
  waiting for transfers between devices: 391 us -> 2.84 us
  blocking collectives: 0 us -> 93.3 us
  starting transfers between devices: 85.7 us -> 9.64 us
  local copies, waits for them, and re-layouts: 21.9 us -> 0.01 us
  between operations: 17.7 us -> 0.67 us
  Pallas kernels: 0 us -> 11.7 us
  other arithmetic: 11.1 us -> 2.23 us
  matrix products: 6.61 us -> 0 us
    reduce_scatter x1 -> x0, waiting for transfers between devices: 231 us -> none  [per_device(): lax.psum_scatter(partial_value, 'bal', scatter_dimension=0, tiled=True)]
    unnamed x3 -> x0, waiting for transfers between devices: 112 us -> none
    ppermute x25 -> x1, starting transfers between devices: 85.6 us -> 1.92 us  [per_device(): total = keep + lax.ppermute(send, 'group', cores)]
    all_to_all x0 -> x1, blocking collectives: none -> 55 us  [per_device(): spread = lax.all_to_all(pieces, 'bal', 0, 0, tiled=True)]
    ppermute x25 -> x1, waiting for transfers between devices: 47.3 us -> 2.84 us  [per_device(): total = keep + lax.ppermute(send, 'group', cores)]
    all_gather x0 -> x1, blocking collectives: none -> 38.4 us  [per_device(): parts = lax.all_gather(part, 'group', axis_index_groups=along)]
    pallas_call x0 -> x3, Pallas kernels: none -> 11.7 us  [the longest x1 9.04 us: per_device(): pl.pallas_call(grad_kernel, out_shape=[shape(bal_count, lines + heads * o...]
    all_to_all x0 -> x1, starting transfers between devices: none -> 7.72 us  [per_device(): home = lax.all_to_all(routed, 'bal', 0, 0, tiled=True)]
  transfers between devices with their start and end apart: 27 -> 2, of which waited for: 13 -> 1; matrix products, arithmetic and copies ran while one was open for 6% -> 0% of each run, Pallas kernels for 0% -> 0%
where the time goes in v1:
time: 121 us; the launch traced here: 120 us
  blocking collectives  93.3 us (77%)
  Pallas kernels  11.7 us (10%)
  starting transfers between devices  9.64 us (8%)
  waiting for transfers between devices  2.84 us (2%)
  other arithmetic  2.23 us (2%)
    all_to_all x1, blocking collectives, per_device(): spread = lax.all_to_all(pieces, 'bal', 0, 0, tiled=True)  55 us
    all_gather x1, blocking collectives, per_device(): parts = lax.all_gather(part, 'group', axis_index_groups=along)  38.4 us
    pallas_call x1, Pallas kernels, per_device(): pl.pallas_call(grad_kernel, out_shape=[shape(bal_count, lines + heads * o...  9.04 us
    all_to_all x1, starting transfers between devices, per_device(): home = lax.all_to_all(routed, 'bal', 0, 0, tiled=True)  7.72 us
    ppermute x1, waiting for transfers between devices, per_device(): total = keep + lax.ppermute(send, 'group', cores)  2.84 us
  transfers between devices with their start and end apart: 2, of which 1 were waited for; matrix products, arithmetic and copies ran while one was open for 0% of the time, Pallas kernels for 0%

profile of v1, /device:TPU:6, one launch (start us, length us, event | category | flops | bytes accessed | tf_op | source)
XLA Modules:
  0.0 120.5 jit_solution(17527890470643636181)
XLA Ops:
  0.6 9.0 %tile_grads.1 = (bf16[32,192,128]{2,1,0:T(8,128)(2,1)}, f32[32,64,128]{2,1,0:T(8,128)}, f32[32,64,128]{2,1,0:T(8,128)}, s32[64]{0:T(128)}, f32[16,32]{1,0:T(8,128)}) custom-call(s32[64]{0:T(128)} %len_ref.1, s32[32]{0:T(128)} %plan_ref.1, bf16[2,128,512]{2,1,0:T(8,128)(2,1)} %refs_0_.1, bf16[2,128,512]{2,1,0:T(8,128)(2,1)} %refs_1_.1, ...), custom_call_target="tpu_custom_call" | custom-call | flops 800000000 | bytes 8000000 | tf_op jit(solution)/shard_map/tile_grads/pallas_call | solution.py:157
  9.7 1.9 %collective-permute-start = (f32[32,64,128]{2,1,0:T(8,128)}, f32[32,64,128]{2,1,0:T(8,128)S(1)}, u32[]{:S(2)}, u32[]{:S(2)}) collective-permute-start(f32[32,64,128]{2,1,0:T(8,128)} %get-tuple-element.22), channel_id=1, source_target_pairs={{0,32},{32,0},{64,96},{96,64},{128,160},{160,128},{192,224},{224,1... | collective-permute-start | bytes 3145736 | tf_op jit(solution)/shard_map/ppermute | solution.py:180
  11.6 2.8 %collective-permute-done = f32[32,64,128]{2,1,0:T(8,128)S(1)} collective-permute-done((f32[32,64,128]{2,1,0:T(8,128)}, f32[32,64,128]{2,1,0:T(8,128)S(1)}, u32[]{:S(2)}, u32[]{:S(2)}) %collective-permute-start) | collective-permute-done | bytes 1048608 | tf_op jit(solution)/shard_map/ppermute | solution.py:180
  14.4 2.2 %fusion = bf16[32,192,128]{2,1,0:T(8,128)(2,1)} fusion(bf16[32,192,128]{2,1,0:T(8,128)(2,1)} %get-tuple-element.20, f32[32,64,128]{2,1,0:T(8,128)} %get-tuple-element.21, f32[32,64,128]{2,1,0:T(8,128)S(1)} %collective-permute-done), kind=kLoop, calls=%fused_computation.1 | loop fusion | flops 524288 | bytes 2621440 | tf_op jit(solution)/shard_map/dynamic_update_slice | solution.py:181
  16.7 0.0 copy-start.2
  16.7 55.0 %all_to_all.10.strips_ref = bf16[32,192,128]{2,1,0:T(8,128)(2,1)S(1)} all-to-all(bf16[32,192,128]{2,1,0:T(8,128)(2,1)} %fusion), channel_id=1, replica_groups=mesh['group'=32,'bal'=32] {'bal'}, dimensions={0} | all-to-all | bytes 3145728 | tf_op jit(solution)/shard_map/all_to_all | solution.py:182
  71.6 0.0 copy-done.2
  71.6 1.7 %routed_order.1 = (bf16[32,128,128]{2,1,0:T(8,128)(2,1)}, f32[64,128]{1,0:T(8,128)S(1)}) custom-call(s32[64]{0:T(128)S(1)} %copy-done.2, bf16[32,192,128]{2,1,0:T(8,128)(2,1)S(1)} %all_to_all.10.strips_ref), custom_call_target="tpu_custom_call" | custom-call | bytes 2000000 | tf_op jit(solution)/shard_map/routed_order/pallas_call | solution.py:183
  73.3 0.0 copy-start
  73.3 0.0 copy-start.1
  73.3 7.7 %all-to-all-start.1 = ((bf16[32,128,128]{2,1,0:T(8,128)(2,1)}), bf16[32,128,128]{2,1,0:T(8,128)(2,1)S(1)}, u32[]{:S(2)}, u32[]{:S(2)}) async-start(bf16[32,128,128]{2,1,0:T(8,128)(2,1)} %get-tuple-element.23), calls=%async_computation.1 | async-start | bytes 2097152 | tf_op jit(solution)/shard_map/all_to_all | solution.py:193
  81.0 38.4 %all-gather = f32[1024,128]{1,0:T(8,128)S(1)} all-gather(f32[64,128]{1,0:T(8,128)S(1)} %get-tuple-element.24), channel_id=2, replica_groups={{0,64,128,192,256,320,384,448,512,576,640,704,768,832,896,960},{32,96,1..., dimensions={0}, use_global_device_ids=true | all-gather | bytes 557056 | tf_op jit(solution)/shard_map/all_gather | solution.py:195
  119.4 0.0 all-to-all-done.1.refs_0_
  119.4 0.0 copy-done
  119.4 0.0 copy-done.1
  119.4 1.0 place_grads.1
Async XLA Ops:
  9.7 4.8 %collective-permute-start = (f32[32,64,128]{2,1,0:T(8,128)}, f32[32,64,128]{2,1,0:T(8,128)S(1)}, u32[]{:S(2)}, u32[]{:S(2)}) collective-permute-start(f32[32,64,128]{2,1,0:T(8,128)} %get-tuple-element.22), channel_id=1, source_target_pairs={{0,32},{32,0},{64,96},{96,64},{128,160},{160,128},{192,224},{224,1... | collective-permute-start | bytes 3145736 | tf_op jit(solution)/shard_map/ppermute | solution.py:180
  16.7 55.0 %copy-start.2 = (s32[64]{0:T(128)S(1)}, s32[64]{0:T(128)}, u32[]{:S(2)}) copy-start(s32[64]{0:T(128)} %get-tuple-element.19.from_ref) | copy-start | bytes 772
  73.3 46.1 %copy-start = (f32[16,32]{1,0:T(8,128)S(1)}, f32[16,32]{1,0:T(8,128)}, u32[]{:S(2)}) copy-start(f32[16,32]{1,0:T(8,128)} %refs_3_.3) | copy-start | bytes 6148
  73.3 46.1 %copy-start.1 = (f32[16,32]{1,0:T(8,128)S(1)}, f32[16,32]{1,0:T(8,128)}, u32[]{:S(2)}) copy-start(f32[16,32]{1,0:T(8,128)} %get-tuple-element.25.refs_2_) | copy-start | bytes 6148
  73.3 46.1 %all-to-all-start.1 = ((bf16[32,128,128]{2,1,0:T(8,128)(2,1)}), bf16[32,128,128]{2,1,0:T(8,128)(2,1)S(1)}, u32[]{:S(2)}, u32[]{:S(2)}) async-start(bf16[32,128,128]{2,1,0:T(8,128)(2,1)} %get-tuple-element.23), calls=%async_computation.1 | async-start | bytes 2097152 | tf_op jit(solution)/shard_map/all_to_all | solution.py:193

commit v2 on v1

--- a/solution.py
+++ b/solution.py
@@ -40,8 +40,6 @@
                 held, other = from_ref[a], from_ref[b]
                 from_ref[a] = other
                 from_ref[b] = held
-    for copy in copies:
-        copy.wait()
     pos, group = lax.axis_index("bal"), lax.axis_index("group")
     rows, width = q.shape[1:]
     strips, share = rows // STRIP, width // HEAD * STRIP
@@ -57,6 +55,9 @@
     for tile in range(slots):
         live = len_ref[pos * slots + tile]
         allowed = (col_ids <= row_ids) & (row_ids < live)
+        if tile == 0:
+            for copy in copies[:3]:
+                copy.wait()
         logits, sigs, atts, mixed = [], [], [], []
         for at in heads_of(width):
             s = dot(q[tile, :, at], k[tile, :, at], 1, 1) * scale
@@ -70,6 +71,9 @@
         centred = o - jnp.mean(o, axis=-1, keepdims=True)
         inv_std = lax.rsqrt(jnp.mean(centred * centred, axis=-1, keepdims=True) + 1e-05)
         normed = centred * inv_std
+        if tile == 0:
+            for copy in copies[3:]:
+                copy.wait()
         gate = u[tile].astype(jnp.float32)
         z_ref[tile] = (normed * gate).astype(jnp.bfloat16)
         row_live = lax.broadcasted_iota(jnp.int32, (rows, 1), 0) < live
@@ -96,10 +100,12 @@
     sum_ref[...] = total.reshape(sum_ref.shape)
     core = group & 1
     own, block = block_ref.shape
+    near_count = sum_ref.shape[0] * block // HEAD
     for out, which in ((keep_ref, core), (send_ref, 1 - core)):
-        half = sum_ref[:, which].reshape(width, width).T
-        for c, at in enumerate(heads_of(width)):
-            out[:, c * own : (c + 1) * own, :] = half[:, at].reshape(count, own, HEAD)
+        for c in range(near_count):
+            picked = [sum_ref[f * near_count + c, which] for f in range(HEAD // block)]
+            half = jnp.concatenate(picked, axis=0).T
+            out[:, c * own : (c + 1) * own, :] = half.reshape(count, own, HEAD)
     wide = w.shape[1]
     pick = lax.broadcasted_iota(jnp.int32, (wide, block), 0) == (
         lax.broadcasted_iota(jnp.int32, (wide, block), 1) + group * block
@@ -129,10 +135,8 @@
                 got = strips_ref[which * strips : (which + 1) * strips, lines, :]
                 outs[which][slot, :, at] = got.reshape(rows, HEAD)
     own, block = outs[4].shape
-    first = (lax.axis_index("group") >> 1) * block
-    lines = pl.ds(pl.multiple_of(first // HEAD * own, own), own)
-    total = jnp.sum(sums_ref[:, lines, :], axis=0)
-    total = pltpu.roll(total, (HEAD - first % HEAD) % HEAD, 1)
+    first = (lax.axis_index("group") >> 1) // (width // HEAD) * block
+    total = pltpu.roll(sums_ref[...], (HEAD - first) % HEAD, 1)
     weight_grad = total[:, :block] * factor
     outs[4][...] = weight_grad
     outs[5][...] = prune_ref[...] - block_ref[...] * weight_grad
@@ -191,8 +195,12 @@
     )(sources, spread)
 
     home = lax.all_to_all(routed, "bal", 0, 0, tiled=True)
-    along = [[2 * z + core for z in range(chips)] for core in range(2)]
-    parts = lax.all_gather(part, "group", axis_index_groups=along)
+    near_by = [[2 * (f * heads + c) + core for c in range(heads)] for f in range(chips // heads) for core in range(2)]
+    far_off = [[2 * (f * heads + c) + core for f in range(chips // heads)] for c in range(heads) for core in range(2)]
+    parts = lax.all_gather(part, "group", axis_index_groups=near_by)
+    near = (lax.axis_index("group") >> 1) % heads
+    parts = jnp.sum(lax.dynamic_slice_in_dim(parts, near * own, own, 1), axis=0)
+    parts = lax.psum(parts, "group", axis_index_groups=far_off)
     tokens_all = group_count * bal_count * slots * rows
     outs = pl.pallas_call(
         lambda *refs: place_kernel(1.0 / math.sqrt(tokens_all), *refs),

time: 121 us -> 116 us (0.959)
  blocking collectives: 93.3 us -> 88.3 us
    all_gather x1, blocking collectives: 38.4 us -> 13.4 us  [per_device(): parts = lax.all_gather(part, 'group', axis_index_groups=near_by)]
    psum x0 -> x1, blocking collectives: none -> 20 us  [per_device(): parts = lax.psum(parts, 'group', axis_index_groups=far_off)]
where the time goes in v2:
time: 116 us; the launch traced here: 115 us
  blocking collectives  88.3 us (76%)
  Pallas kernels  11.3 us (10%)
  starting transfers between devices  9.64 us (8%)
  waiting for transfers between devices  2.84 us (2%)
  other arithmetic  2.22 us (2%)
    all_to_all x1, blocking collectives, per_device(): spread = lax.all_to_all(pieces, 'bal', 0, 0, tiled=True)  55 us
    psum x1, blocking collectives, per_device(): parts = lax.psum(parts, 'group', axis_index_groups=far_off)  20 us
    all_gather x1, blocking collectives, per_device(): parts = lax.all_gather(part, 'group', axis_index_groups=near_by)  13.4 us
    pallas_call x1, Pallas kernels, per_device(): pl.pallas_call(grad_kernel, out_shape=[shape(bal_count, lines + heads * o...  8.66 us
    all_to_all x1, starting transfers between devices, per_device(): home = lax.all_to_all(routed, 'bal', 0, 0, tiled=True)  7.72 us
    ppermute x1, waiting for transfers between devices, per_device(): total = keep + lax.ppermute(send, 'group', cores)  2.84 us
  transfers between devices with their start and end apart: 2, of which 1 were waited for; matrix products, arithmetic and copies ran while one was open for 0% of the time, Pallas kernels for 0%

profile of v2, /device:TPU:6, one launch (start us, length us, event | category | flops | bytes accessed | tf_op | source)
XLA Modules:
  0.0 115.1 jit_solution(9031502063236778930)
XLA Ops:
  0.6 8.7 %tile_grads.1 = (bf16[32,192,128]{2,1,0:T(8,128)(2,1)}, f32[32,64,128]{2,1,0:T(8,128)}, f32[32,64,128]{2,1,0:T(8,128)}, s32[64]{0:T(128)}, f32[16,32]{1,0:T(8,128)}) custom-call(s32[64]{0:T(128)} %len_ref.1, s32[32]{0:T(128)} %plan_ref.1, bf16[2,128,512]{2,1,0:T(8,128)(2,1)} %refs_0_.1, bf16[2,128,512]{2,1,0:T(8,128)(2,1)} %refs_1_.1, ...), custom_call_target="tpu_custom_call" | custom-call | flops 800000000 | bytes 8000000 | tf_op jit(solution)/shard_map/tile_grads/pallas_call | solution.py:161
  9.3 1.9 %collective-permute-start = (f32[32,64,128]{2,1,0:T(8,128)}, f32[32,64,128]{2,1,0:T(8,128)S(1)}, u32[]{:S(2)}, u32[]{:S(2)}) collective-permute-start(f32[32,64,128]{2,1,0:T(8,128)} %get-tuple-element.22), channel_id=1, source_target_pairs={{0,32},{32,0},{64,96},{96,64},{128,160},{160,128},{192,224},{224,1... | collective-permute-start | bytes 3145736 | tf_op jit(solution)/shard_map/ppermute | solution.py:184
  11.2 2.8 %collective-permute-done = f32[32,64,128]{2,1,0:T(8,128)S(1)} collective-permute-done((f32[32,64,128]{2,1,0:T(8,128)}, f32[32,64,128]{2,1,0:T(8,128)S(1)}, u32[]{:S(2)}, u32[]{:S(2)}) %collective-permute-start) | collective-permute-done | bytes 1048608 | tf_op jit(solution)/shard_map/ppermute | solution.py:184
  14.1 2.2 %fusion = bf16[32,192,128]{2,1,0:T(8,128)(2,1)} fusion(bf16[32,192,128]{2,1,0:T(8,128)(2,1)} %get-tuple-element.20, f32[32,64,128]{2,1,0:T(8,128)} %get-tuple-element.21, f32[32,64,128]{2,1,0:T(8,128)S(1)} %collective-permute-done), kind=kLoop, calls=%fused_computation.1 | loop fusion | flops 524288 | bytes 2621440 | tf_op jit(solution)/shard_map/dynamic_update_slice | solution.py:185
  16.3 0.0 copy-start.2
  16.3 55.0 %all_to_all.10.strips_ref = bf16[32,192,128]{2,1,0:T(8,128)(2,1)S(1)} all-to-all(bf16[32,192,128]{2,1,0:T(8,128)(2,1)} %fusion), channel_id=1, replica_groups=mesh['group'=32,'bal'=32] {'bal'}, dimensions={0} | all-to-all | bytes 3145728 | tf_op jit(solution)/shard_map/all_to_all | solution.py:186
  71.2 0.0 copy-done.2
  71.2 1.7 %routed_order.1 = (bf16[32,128,128]{2,1,0:T(8,128)(2,1)}, f32[64,128]{1,0:T(8,128)S(1)}) custom-call(s32[64]{0:T(128)S(1)} %copy-done.2, bf16[32,192,128]{2,1,0:T(8,128)(2,1)S(1)} %all_to_all.10.strips_ref), custom_call_target="tpu_custom_call" | custom-call | bytes 2000000 | tf_op jit(solution)/shard_map/routed_order/pallas_call | solution.py:187
  72.9 0.0 copy-start
  72.9 0.0 copy-start.1
  72.9 7.7 %all-to-all-start.1 = ((bf16[32,128,128]{2,1,0:T(8,128)(2,1)}), bf16[32,128,128]{2,1,0:T(8,128)(2,1)S(1)}, u32[]{:S(2)}, u32[]{:S(2)}) async-start(bf16[32,128,128]{2,1,0:T(8,128)(2,1)} %get-tuple-element.23), calls=%async_computation.1 | async-start | bytes 2097152 | tf_op jit(solution)/shard_map/all_to_all | solution.py:197
  80.7 13.4 %all-gather = f32[256,128]{1,0:T(8,128)S(1)} all-gather(f32[64,128]{1,0:T(8,128)S(1)} %get-tuple-element.24), channel_id=2, replica_groups={{0,64,128,192},{32,96,160,224},{256,320,384,448},{288,352,416,480},{512..., dimensions={0}, use_global_device_ids=true | all-gather | bytes 163840 | tf_op jit(solution)/shard_map/all_gather | solution.py:200
  94.1 20.0 %psum.7.refs_1_ = f32[16,128]{1,0:T(8,128)S(1)} all-reduce(f32[16,128]{1,0:T(8,128)S(1)} %dynamic-slice_reduce_fusion), channel_id=1, replica_groups={{0,256,512,768},{32,288,544,800},{64,320,576,832},{96,352,608,864},{128..., use_global_device_ids=true, to_apply=%region_1.2 | all-reduce | flops 2048 | bytes 16384 | tf_op jit(solution)/shard_map/psum | solution.py:203
  114.0 0.0 all-to-all-done.1.refs_0_
  114.0 0.0 copy-done
  114.0 0.0 copy-done.1
  114.1 1.0 place_grads.1
  (1 shorter events, 0.0 us)
Async XLA Ops:
  9.3 4.8 %collective-permute-start = (f32[32,64,128]{2,1,0:T(8,128)}, f32[32,64,128]{2,1,0:T(8,128)S(1)}, u32[]{:S(2)}, u32[]{:S(2)}) collective-permute-start(f32[32,64,128]{2,1,0:T(8,128)} %get-tuple-element.22), channel_id=1, source_target_pairs={{0,32},{32,0},{64,96},{96,64},{128,160},{160,128},{192,224},{224,1... | collective-permute-start | bytes 3145736 | tf_op jit(solution)/shard_map/ppermute | solution.py:184
  16.3 55.0 %copy-start.2 = (s32[64]{0:T(128)S(1)}, s32[64]{0:T(128)}, u32[]{:S(2)}) copy-start(s32[64]{0:T(128)} %get-tuple-element.19.from_ref) | copy-start | bytes 772
  72.9 41.1 %copy-start = (f32[16,32]{1,0:T(8,128)S(1)}, f32[16,32]{1,0:T(8,128)}, u32[]{:S(2)}) copy-start(f32[16,32]{1,0:T(8,128)} %refs_3_.3) | copy-start | bytes 6148
  72.9 41.1 %copy-start.1 = (f32[16,32]{1,0:T(8,128)S(1)}, f32[16,32]{1,0:T(8,128)}, u32[]{:S(2)}) copy-start(f32[16,32]{1,0:T(8,128)} %get-tuple-element.25.refs_2_) | copy-start | bytes 6148
  72.9 41.1 %all-to-all-start.1 = ((bf16[32,128,128]{2,1,0:T(8,128)(2,1)}), bf16[32,128,128]{2,1,0:T(8,128)(2,1)S(1)}, u32[]{:S(2)}, u32[]{:S(2)}) async-start(bf16[32,128,128]{2,1,0:T(8,128)(2,1)} %get-tuple-element.23), calls=%async_computation.1 | async-start | bytes 2097152 | tf_op jit(solution)/shard_map/all_to_all | solution.py:197

commit v3 on v2

--- a/solution.py
+++ b/solution.py
@@ -105,7 +105,7 @@
         for c in range(near_count):
             picked = [sum_ref[f * near_count + c, which] for f in range(HEAD // block)]
             half = jnp.concatenate(picked, axis=0).T
-            out[:, c * own : (c + 1) * own, :] = half.reshape(count, own, HEAD)
+            out[:, c * own : (c + 1) * own, :] = half.reshape(count, own, HEAD).astype(out.dtype)
     wide = w.shape[1]
     pick = lax.broadcasted_iota(jnp.int32, (wide, block), 0) == (
         lax.broadcasted_iota(jnp.int32, (wide, block), 1) + group * block
@@ -157,13 +157,12 @@
     def shape(*dims, kind=jnp.float32):
         return jax.ShapeDtypeStruct(dims, kind)
 
-    half = shape(bal_count, heads * own, HEAD)
     pieces, keep, send, sources, weight_block = pl.pallas_call(
         grad_kernel,
         out_shape=[
             shape(bal_count, lines + heads * own, HEAD, kind=jnp.bfloat16),
-            half,
-            half,
+            shape(bal_count, heads * own, HEAD),
+            shape(bal_count, heads * own, HEAD, kind=jnp.bfloat16),
             shape(bal_count * slots, kind=jnp.int32),
             shape(own, block),
         ],
@@ -181,7 +180,7 @@
     )(lengths, plan, *far)
 
     cores = [(i, i ^ 1) for i in range(group_count)]
-    total = keep + lax.ppermute(send, "group", cores)
+    total = keep + lax.ppermute(send, "group", cores).astype(jnp.float32)
     pieces = lax.dynamic_update_slice(pieces, total.astype(pieces.dtype), (0, lines, 0))
     spread = lax.all_to_all(pieces, "bal", 0, 0, tiled=True)
     routed, part = pl.pallas_call(

time: 116 us -> 114 us (0.983)
  no operation moved by 1% of the time
where the time goes in v3:
time: 114 us
  blocking collectives  88.3 us (77%)
  Pallas kernels  11 us (10%)
  starting transfers between devices  9.64 us (8%)
  other arithmetic  2.21 us (2%)
  waiting for transfers between devices  2.09 us (2%)
    all_to_all x1, blocking collectives, per_device(): spread = lax.all_to_all(pieces, 'bal', 0, 0, tiled=True)  55 us
    psum x1, blocking collectives, per_device(): parts = lax.psum(parts, 'group', axis_index_groups=far_off)  20 us
    all_gather x1, blocking collectives, per_device(): parts = lax.all_gather(part, 'group', axis_index_groups=near_by)  13.4 us
    pallas_call x1, Pallas kernels, per_device(): pl.pallas_call(grad_kernel, out_shape=[shape(bal_count, lines + heads * o...  8.34 us
    all_to_all x1, starting transfers between devices, per_device(): home = lax.all_to_all(routed, 'bal', 0, 0, tiled=True)  7.72 us
  transfers between devices with their start and end apart: 2, of which 1 were waited for; matrix products, arithmetic and copies ran while one was open for 0% of the time, Pallas kernels for 0%

profile of v3, /device:TPU:6, one launch (start us, length us, event | category | flops | bytes accessed | tf_op | source)
XLA Modules:
  0.0 114.0 jit_solution(13354713793475806468)
XLA Ops:
  0.6 8.3 %tile_grads.1 = (bf16[32,192,128]{2,1,0:T(8,128)(2,1)}, f32[32,64,128]{2,1,0:T(8,128)}, bf16[32,64,128]{2,1,0:T(8,128)(2,1)}, s32[64]{0:T(128)}, f32[16,32]{1,0:T(8,128)}) custom-call(s32[64]{0:T(128)} %len_ref.1, s32[32]{0:T(128)} %plan_ref.1, bf16[2,128,512]{2,1,0:T(8,128)(2,1)} %refs_0_.1, bf16[2,128,512]{2,1,0:T(8,128)(2,1)} %refs_1_.1, ...), custom_call_target="tpu_custom_call" | custom-call | flops 800000000 | bytes 8000000 | tf_op jit(solution)/shard_map/tile_grads/pallas_call | solution.py:160
  9.0 1.9 %collective-permute-start = (bf16[32,64,128]{2,1,0:T(8,128)(2,1)}, bf16[32,64,128]{2,1,0:T(8,128)(2,1)S(1)}, u32[]{:S(2)}, u32[]{:S(2)}) collective-permute-start(bf16[32,64,128]{2,1,0:T(8,128)(2,1)} %get-tuple-element.22), channel_id=1, source_target_pairs={{0,32},{32,0},{64,96},{96,64},{128,160},{160,128},{192,224},{224,1... | collective-permute-start | bytes 1572872 | tf_op jit(solution)/shard_map/ppermute | solution.py:183
  10.9 2.1 %collective-permute-done = bf16[32,64,128]{2,1,0:T(8,128)(2,1)S(1)} collective-permute-done((bf16[32,64,128]{2,1,0:T(8,128)(2,1)}, bf16[32,64,128]{2,1,0:T(8,128)(2,1)S(1)}, u32[]{:S(2)}, u32[]{:S(2)}) %collective-permute-start) | collective-permute-done | bytes 524320 | tf_op jit(solution)/shard_map/ppermute | solution.py:183
  13.0 2.2 %fusion = bf16[32,192,128]{2,1,0:T(8,128)(2,1)} fusion(bf16[32,192,128]{2,1,0:T(8,128)(2,1)} %get-tuple-element.20, f32[32,64,128]{2,1,0:T(8,128)} %get-tuple-element.21, bf16[32,64,128]{2,1,0:T(8,128)(2,1)S(1)} %collective-permute-done), kind=kLoop, calls=%fused_computation.1 | loop fusion | flops 786432 | bytes 2097152 | tf_op jit(solution)/shard_map/dynamic_update_slice | solution.py:184
  15.2 0.0 copy-start.2
  15.2 55.0 %all_to_all.10.strips_ref = bf16[32,192,128]{2,1,0:T(8,128)(2,1)S(1)} all-to-all(bf16[32,192,128]{2,1,0:T(8,128)(2,1)} %fusion), channel_id=1, replica_groups=mesh['group'=32,'bal'=32] {'bal'}, dimensions={0} | all-to-all | bytes 3145728 | tf_op jit(solution)/shard_map/all_to_all | solution.py:185
  70.2 0.0 copy-done.2
  70.2 1.7 %routed_order.1 = (bf16[32,128,128]{2,1,0:T(8,128)(2,1)}, f32[64,128]{1,0:T(8,128)S(1)}) custom-call(s32[64]{0:T(128)S(1)} %copy-done.2, bf16[32,192,128]{2,1,0:T(8,128)(2,1)S(1)} %all_to_all.10.strips_ref), custom_call_target="tpu_custom_call" | custom-call | bytes 2000000 | tf_op jit(solution)/shard_map/routed_order/pallas_call | solution.py:186
  71.8 0.0 copy-start
  71.8 0.0 copy-start.1
  71.8 7.7 %all-to-all-start.1 = ((bf16[32,128,128]{2,1,0:T(8,128)(2,1)}), bf16[32,128,128]{2,1,0:T(8,128)(2,1)S(1)}, u32[]{:S(2)}, u32[]{:S(2)}) async-start(bf16[32,128,128]{2,1,0:T(8,128)(2,1)} %get-tuple-element.23), calls=%async_computation.1 | async-start | bytes 2097152 | tf_op jit(solution)/shard_map/all_to_all | solution.py:196
  79.6 13.4 %all-gather = f32[256,128]{1,0:T(8,128)S(1)} all-gather(f32[64,128]{1,0:T(8,128)S(1)} %get-tuple-element.24), channel_id=2, replica_groups={{0,64,128,192},{32,96,160,224},{256,320,384,448},{288,352,416,480},{512..., dimensions={0}, use_global_device_ids=true | all-gather | bytes 163840 | tf_op jit(solution)/shard_map/all_gather | solution.py:199
  93.0 20.0 %psum.7.refs_1_ = f32[16,128]{1,0:T(8,128)S(1)} all-reduce(f32[16,128]{1,0:T(8,128)S(1)} %dynamic-slice_reduce_fusion), channel_id=1, replica_groups={{0,256,512,768},{32,288,544,800},{64,320,576,832},{96,352,608,864},{128..., use_global_device_ids=true, to_apply=%region_1.2 | all-reduce | flops 2048 | bytes 16384 | tf_op jit(solution)/shard_map/psum | solution.py:202
  112.9 0.0 all-to-all-done.1.refs_0_
  113.0 0.0 copy-done
  113.0 0.0 copy-done.1
  113.0 1.0 place_grads.1
  (1 shorter events, 0.0 us)
Async XLA Ops:
  9.0 4.0 %collective-permute-start = (bf16[32,64,128]{2,1,0:T(8,128)(2,1)}, bf16[32,64,128]{2,1,0:T(8,128)(2,1)S(1)}, u32[]{:S(2)}, u32[]{:S(2)}) collective-permute-start(bf16[32,64,128]{2,1,0:T(8,128)(2,1)} %get-tuple-element.22), channel_id=1, source_target_pairs={{0,32},{32,0},{64,96},{96,64},{128,160},{160,128},{192,224},{224,1... | collective-permute-start | bytes 1572872 | tf_op jit(solution)/shard_map/ppermute | solution.py:183
  15.2 55.0 %copy-start.2 = (s32[64]{0:T(128)S(1)}, s32[64]{0:T(128)}, u32[]{:S(2)}) copy-start(s32[64]{0:T(128)} %get-tuple-element.19.from_ref) | copy-start | bytes 772
  71.8 41.1 %copy-start = (f32[16,32]{1,0:T(8,128)S(1)}, f32[16,32]{1,0:T(8,128)}, u32[]{:S(2)}) copy-start(f32[16,32]{1,0:T(8,128)} %refs_3_.3) | copy-start | bytes 6148
  71.8 41.1 %copy-start.1 = (f32[16,32]{1,0:T(8,128)S(1)}, f32[16,32]{1,0:T(8,128)}, u32[]{:S(2)}) copy-start(f32[16,32]{1,0:T(8,128)} %get-tuple-element.25.refs_2_) | copy-start | bytes 6148
  71.8 41.1 %all-to-all-start.1 = ((bf16[32,128,128]{2,1,0:T(8,128)(2,1)}), bf16[32,128,128]{2,1,0:T(8,128)(2,1)S(1)}, u32[]{:S(2)}, u32[]{:S(2)}) async-start(bf16[32,128,128]{2,1,0:T(8,128)(2,1)} %get-tuple-element.23), calls=%async_computation.1 | async-start | bytes 2097152 | tf_op jit(solution)/shard_map/all_to_all | solution.py:196

commit v4 on v3

--- a/solution.py
+++ b/solution.py
@@ -196,9 +196,10 @@
     home = lax.all_to_all(routed, "bal", 0, 0, tiled=True)
     near_by = [[2 * (f * heads + c) + core for c in range(heads)] for f in range(chips // heads) for core in range(2)]
     far_off = [[2 * (f * heads + c) + core for f in range(chips // heads)] for c in range(heads) for core in range(2)]
-    parts = lax.all_gather(part, "group", axis_index_groups=near_by)
+    parts = lax.all_gather(part.astype(jnp.bfloat16), "group", axis_index_groups=near_by)
     near = (lax.axis_index("group") >> 1) % heads
-    parts = jnp.sum(lax.dynamic_slice_in_dim(parts, near * own, own, 1), axis=0)
+    parts = lax.dynamic_slice_in_dim(parts, near * own, own, 1).astype(jnp.float32)
+    parts = jnp.sum(parts, axis=0)
     parts = lax.psum(parts, "group", axis_index_groups=far_off)
     tokens_all = group_count * bal_count * slots * rows
     outs = pl.pallas_call(

time: 114 us -> 114 us (level)
  no operation moved by 1% of the time
where the time goes in v4:
time: 114 us
  blocking collectives  88 us (77%)
  Pallas kernels  11 us (10%)
  starting transfers between devices  9.51 us (8%)
  other arithmetic  2.21 us (2%)
  waiting for transfers between devices  2.09 us (2%)
    all_to_all x1, blocking collectives, per_device(): spread = lax.all_to_all(pieces, 'bal', 0, 0, tiled=True)  55 us
    psum x1, blocking collectives, per_device(): parts = lax.psum(parts, 'group', axis_index_groups=far_off)  19.9 us
    all_gather x1, blocking collectives, per_device(): lax.all_gather(part.astype(jnp.bfloat16), 'group', axis_index_groups=near...  13.1 us
    pallas_call x1, Pallas kernels, per_device(): pl.pallas_call(grad_kernel, out_shape=[shape(bal_count, lines + heads * o...  8.34 us
    all_to_all x1, starting transfers between devices, per_device(): home = lax.all_to_all(routed, 'bal', 0, 0, tiled=True)  7.59 us
  transfers between devices with their start and end apart: 2, of which 1 were waited for; matrix products, arithmetic and copies ran while one was open for 0% of the time, Pallas kernels for 0%

profile of v4, /device:TPU:6, one launch (start us, length us, event | category | flops | bytes accessed | tf_op | source)
XLA Modules:
  0.0 113.6 jit_solution(10511241498558042873)
XLA Ops:
  0.6 8.3 %tile_grads.1 = (bf16[32,192,128]{2,1,0:T(8,128)(2,1)}, f32[32,64,128]{2,1,0:T(8,128)}, bf16[32,64,128]{2,1,0:T(8,128)(2,1)}, s32[64]{0:T(128)}, f32[16,32]{1,0:T(8,128)}) custom-call(s32[64]{0:T(128)} %len_ref.1, s32[32]{0:T(128)} %plan_ref.1, bf16[2,128,512]{2,1,0:T(8,128)(2,1)} %refs_0_.1, bf16[2,128,512]{2,1,0:T(8,128)(2,1)} %refs_1_.1, ...), custom_call_target="tpu_custom_call" | custom-call | flops 800000000 | bytes 8000000 | tf_op jit(solution)/shard_map/tile_grads/pallas_call | solution.py:160
  9.0 1.9 %collective-permute-start = (bf16[32,64,128]{2,1,0:T(8,128)(2,1)}, bf16[32,64,128]{2,1,0:T(8,128)(2,1)S(1)}, u32[]{:S(2)}, u32[]{:S(2)}) collective-permute-start(bf16[32,64,128]{2,1,0:T(8,128)(2,1)} %get-tuple-element.22), channel_id=1, source_target_pairs={{0,32},{32,0},{64,96},{96,64},{128,160},{160,128},{192,224},{224,1... | collective-permute-start | bytes 1572872 | tf_op jit(solution)/shard_map/ppermute | solution.py:183
  10.9 2.1 %collective-permute-done = bf16[32,64,128]{2,1,0:T(8,128)(2,1)S(1)} collective-permute-done((bf16[32,64,128]{2,1,0:T(8,128)(2,1)}, bf16[32,64,128]{2,1,0:T(8,128)(2,1)S(1)}, u32[]{:S(2)}, u32[]{:S(2)}) %collective-permute-start) | collective-permute-done | bytes 524320 | tf_op jit(solution)/shard_map/ppermute | solution.py:183
  13.0 2.2 %fusion = bf16[32,192,128]{2,1,0:T(8,128)(2,1)} fusion(bf16[32,192,128]{2,1,0:T(8,128)(2,1)} %get-tuple-element.20, f32[32,64,128]{2,1,0:T(8,128)} %get-tuple-element.21, bf16[32,64,128]{2,1,0:T(8,128)(2,1)S(1)} %collective-permute-done), kind=kLoop, calls=%fused_computation.1 | loop fusion | flops 786432 | bytes 2097152 | tf_op jit(solution)/shard_map/dynamic_update_slice | solution.py:184
  15.2 0.0 copy-start.2
  15.2 55.0 %all_to_all.10.strips_ref = bf16[32,192,128]{2,1,0:T(8,128)(2,1)S(1)} all-to-all(bf16[32,192,128]{2,1,0:T(8,128)(2,1)} %fusion), channel_id=1, replica_groups=mesh['group'=32,'bal'=32] {'bal'}, dimensions={0} | all-to-all | bytes 3145728 | tf_op jit(solution)/shard_map/all_to_all | solution.py:185
  70.2 0.0 copy-done.2
  70.2 0.0 copy-start
  70.2 0.0 copy-start.1
  70.2 1.7 %routed_order.1 = (bf16[32,128,128]{2,1,0:T(8,128)(2,1)}, f32[64,128]{1,0:T(8,128)S(1)}) custom-call(s32[64]{0:T(128)S(1)} %copy-done.2, bf16[32,192,128]{2,1,0:T(8,128)(2,1)S(1)} %all_to_all.10.strips_ref), custom_call_target="tpu_custom_call" | custom-call | bytes 2000000 | tf_op jit(solution)/shard_map/routed_order/pallas_call | solution.py:186
  71.8 7.6 %all-to-all-start.1 = ((bf16[32,128,128]{2,1,0:T(8,128)(2,1)}), bf16[32,128,128]{2,1,0:T(8,128)(2,1)S(1)}, u32[]{:S(2)}, u32[]{:S(2)}) async-start(bf16[32,128,128]{2,1,0:T(8,128)(2,1)} %get-tuple-element.23), calls=%async_computation.1 | async-start | bytes 2097152 | tf_op jit(solution)/shard_map/all_to_all | solution.py:196
  79.5 13.1 %all-gather = bf16[256,128]{1,0:T(8,128)(2,1)S(1)} all-gather(bf16[64,128]{1,0:T(8,128)(2,1)S(1)} %convert_element_type.14), channel_id=2, replica_groups={{0,64,128,192},{32,96,160,224},{256,320,384,448},{288,352,416,480},{512..., dimensions={0}, use_global_device_ids=true | all-gather | bytes 81920 | tf_op jit(solution)/shard_map/all_gather | solution.py:199
  92.6 19.9 %psum.7.refs_1_ = f32[16,128]{1,0:T(8,128)S(1)} all-reduce(f32[16,128]{1,0:T(8,128)S(1)} %convert_reduce_fusion), channel_id=1, replica_groups={{0,256,512,768},{32,288,544,800},{64,320,576,832},{96,352,608,864},{128..., use_global_device_ids=true, to_apply=%region_1.2 | all-reduce | flops 2048 | bytes 16384 | tf_op jit(solution)/shard_map/psum | solution.py:203
  112.5 0.0 all-to-all-done.1.refs_0_
  112.5 0.0 copy-done
  112.5 0.0 copy-done.1
  112.6 1.0 place_grads.1
  (2 shorter events, 0.0 us)
Async XLA Ops:
  9.0 4.0 %collective-permute-start = (bf16[32,64,128]{2,1,0:T(8,128)(2,1)}, bf16[32,64,128]{2,1,0:T(8,128)(2,1)S(1)}, u32[]{:S(2)}, u32[]{:S(2)}) collective-permute-start(bf16[32,64,128]{2,1,0:T(8,128)(2,1)} %get-tuple-element.22), channel_id=1, source_target_pairs={{0,32},{32,0},{64,96},{96,64},{128,160},{160,128},{192,224},{224,1... | collective-permute-start | bytes 1572872 | tf_op jit(solution)/shard_map/ppermute | solution.py:183
  15.2 55.0 %copy-start.2 = (s32[64]{0:T(128)S(1)}, s32[64]{0:T(128)}, u32[]{:S(2)}) copy-start(s32[64]{0:T(128)} %get-tuple-element.19.from_ref) | copy-start | bytes 772
  70.2 42.4 %copy-start = (f32[16,32]{1,0:T(8,128)S(1)}, f32[16,32]{1,0:T(8,128)}, u32[]{:S(2)}) copy-start(f32[16,32]{1,0:T(8,128)} %refs_3_.3) | copy-start | bytes 6148
  70.2 42.4 %copy-start.1 = (f32[16,32]{1,0:T(8,128)S(1)}, f32[16,32]{1,0:T(8,128)}, u32[]{:S(2)}) copy-start(f32[16,32]{1,0:T(8,128)} %get-tuple-element.25.refs_2_) | copy-start | bytes 6148
  71.8 40.7 %all-to-all-start.1 = ((bf16[32,128,128]{2,1,0:T(8,128)(2,1)}), bf16[32,128,128]{2,1,0:T(8,128)(2,1)S(1)}, u32[]{:S(2)}, u32[]{:S(2)}) async-start(bf16[32,128,128]{2,1,0:T(8,128)(2,1)} %get-tuple-element.23), calls=%async_computation.1 | async-start | bytes 2097152 | tf_op jit(solution)/shard_map/all_to_all | solution.py:196
